TPU v7x, 512 devices: a whole 4x4x16 slice. The times are simulated.
512 devices in a mesh: bt: 64 (over z, x), ch: 8 (over y, core).
Axes of the slice: x: 4, y: 4, z: 16, core: 2. Of those that a mesh axis runs over, the one named last changes fastest.
Arguments:
- visibility: float32 [2, 4, 64, 16384], P(None, None, 'ch', 'bt'), may hold values from -6 to 6
- cell_offset: float32 [2, 4, 64, 16384], P(None, None, 'ch', 'bt'), may hold values from 2 to 30
- station_gain: float32 [2, 64, 512], P(None, 'ch'), may hold values from 0.1 to 1.9
- stations: int32 [16384, 2], P('bt'), may hold values from 0 to 511, all different within a row
- row_band: int32 [16384, 1], replicated, may hold values from 0 to 63; in each aligned block of 32 rows (0 to 31, 32 to 63, ...) at most 2 rows name the same one
- tile_offset: int32 [16384], replicated, may hold values from 0 to 127
Outputs:
- sky_image: float32 [2, 8192, 8192], P(None, ('bt', 'ch'))
Inputs may be any that keep to these rules, and one draw needn't show every extreme that they name: `row_band`: in each aligned run of 32 blocks (one bt index's blocks of one column band) no row band is named by more than 2 blocks. The two stations of a block differ.
All inputs are finite; a program needn't handle non-finite values.
Results may differ from a plain program's by a relative error of at most 0.0003.
Values sent between devices are 32-bit elements; how exact they have to be, the bound alone decides.
A program may use at most 64 MiB of HBM per device.

v0:
```python
import math

import jax
import jax.numpy as jnp
from jax import lax
from jax.sharding import PartitionSpec as P

SUB = 32
G1 = 64
G2 = 128
TSLOT = 4
CHANNELS = 64


highest = lax.Precision.HIGHEST
full_turn = 2.0 * math.pi


def complex_einsum(form, left_side, right_side):
    real_part = jnp.einsum(form, left_side[0], right_side[0], precision=highest) - jnp.einsum(
        form, left_side[1], right_side[1], precision=highest
    )
    imag_part = jnp.einsum(form, left_side[0], right_side[1], precision=highest) + jnp.einsum(
        form, left_side[1], right_side[0], precision=highest
    )
    return jnp.stack([real_part, imag_part])


def complex_product(left_side, right_side):
    return jnp.stack(
        [
            left_side[0] * right_side[0] - left_side[1] * right_side[1],
            left_side[0] * right_side[1] + left_side[1] * right_side[0],
        ]
    )


def centred_offsets(length):
    return (jnp.arange(length, dtype=jnp.float32) - length // 2) / length


def phasor_pair(coords, length):
    angles = (full_turn * centred_offsets(length))[None, :, None] * coords[:, None, :]
    return jnp.stack([jnp.cos(angles), jnp.sin(angles)])


def tile_table(length):
    positions = jnp.arange(length, dtype=jnp.int32)
    product = positions[:, None] * (positions[None, :] - length // 2) % length
    angles = -full_turn * product.astype(jnp.float32) / length
    centred = centred_offsets(length)
    tapers = jnp.exp(-4.0 * centred * centred) / math.sqrt(length)
    return jnp.stack([jnp.cos(angles) * tapers[None, :], jnp.sin(angles) * tapers[None, :]])


def weighted_vis(visibility, gain_first, gain_second):
    product_real = gain_first[0] * gain_second[0] + gain_first[1] * gain_second[1]
    product_imag = gain_first[1] * gain_second[0] - gain_first[0] * gain_second[1]
    real_part = visibility[0] * product_real[None] - visibility[1] * product_imag[None]
    imag_part = visibility[0] * product_imag[None] + visibility[1] * product_real[None]
    return jnp.stack([real_part, imag_part])


def image_subgrids(weighted, coords):
    phase_first = phasor_pair(coords[0], SUB)
    phase_second = phasor_pair(coords[1], SUB)
    scaled = jnp.stack(
        [
            weighted[0][:, None, :] * phase_first[0] - weighted[1][:, None, :] * phase_first[1],
            weighted[0][:, None, :] * phase_first[1] + weighted[1][:, None, :] * phase_first[0],
        ]
    )
    return complex_einsum("klb,kmb->lmb", scaled, phase_second)


def to_tiles(subgrid_image):
    factor_table = tile_table(SUB)
    partial_value = complex_einsum("pl,lmb->pmb", factor_table, subgrid_image)
    return complex_einsum("qm,pmb->pqb", factor_table, partial_value)


def dft_table(length):
    positions = jnp.arange(length, dtype=jnp.int32)
    angles = (
        full_turn * (positions[:, None] * positions[None, :] % length).astype(jnp.float32) / length
    )
    return jnp.stack([jnp.cos(angles), jnp.sin(angles)])


def twiddle_table(outer_length, inner_length):
    full_length = outer_length * inner_length
    outer_index = jnp.arange(outer_length, dtype=jnp.int32)
    inner_index = jnp.arange(inner_length, dtype=jnp.int32)
    angles = (
        full_turn
        * (outer_index[:, None] * inner_index[None, :] % full_length).astype(jnp.float32)
        / full_length
    )
    return jnp.stack([jnp.cos(angles), jnp.sin(angles)])


def transform_rows(cells):
    columns = cells.shape[2]
    blocked = cells.reshape(2, G1, G2, columns)
    section_one = complex_einsum("kn,nmc->kmc", dft_table(G1), blocked)
    section_one = complex_product(section_one, twiddle_table(G1, G2)[:, :, :, None])
    section_two = complex_einsum("mn,knc->mkc", dft_table(G2), section_one)
    return section_two.reshape(2, G1 * G2, columns)


def transform_columns(cells):
    row_count = cells.shape[1]
    blocked = cells.reshape(2, row_count, G1, G2)
    section_one = complex_einsum("kn,rnm->rkm", dft_table(G1), blocked)
    section_one = complex_product(section_one, twiddle_table(G1, G2)[:, None, :, :])
    section_two = complex_einsum("mn,rkn->rmk", dft_table(G2), section_one)
    return section_two.reshape(2, row_count, G1 * G2)


def band_ranks(bands, band_count):
    marked = (bands[:, :, None] == jnp.arange(band_count, dtype=jnp.int32)[None, None, :]).astype(
        jnp.int32
    )
    before = jnp.cumsum(marked, axis=1) - marked
    return jnp.sum(before * marked, axis=2)


def station_pick(chosen, station_count):
    return (jnp.arange(station_count, dtype=jnp.int32)[:, None] == chosen[None, :]).astype(
        jnp.float32
    )


def shards(visibility, cell_offset, station_gain, stations, row_band, tile_offset):
    bt_count = lax.axis_size("bt")
    ch_count = lax.axis_size("ch")
    bt_position = lax.axis_index("bt")
    ch_position = lax.axis_index("ch")
    blocks = visibility.shape[3]
    per_band = blocks // ch_count
    tiles_across = G1 * G2 // SUB
    rows_band = tiles_across // bt_count
    cols_band = tiles_across // ch_count
    capacity = max(2, 2 * blocks // (ch_count * bt_count))
    slot_count = bt_count * capacity
    station_count = station_gain.shape[2]
    gain_first = jnp.einsum(
        "xcs,sb->xcb", station_gain, station_pick(stations[:, 0], station_count), precision=highest
    )
    gain_second = jnp.einsum(
        "xcs,sb->xcb", station_gain, station_pick(stations[:, 1], station_count), precision=highest
    )
    weighted_full = weighted_vis(visibility, gain_first, gain_second)
    band_weights, band_coords = (
        lax.all_to_all(weighted_full, "ch", split_axis=3, concat_axis=2, tiled=True),
        lax.all_to_all(cell_offset, "ch", split_axis=3, concat_axis=2, tiled=True),
    )
    tile_stack = to_tiles(
        image_subgrids(band_weights.reshape(2, -1, per_band), band_coords.reshape(2, -1, per_band))
    )
    band_table = row_band.reshape(bt_count, blocks)
    band_part = lax.dynamic_slice_in_dim(band_table, ch_position * per_band, per_band, 1)
    rank_part = band_ranks(band_part, bt_count)
    own_band = lax.dynamic_index_in_dim(band_part, bt_position, 0, keepdims=False)
    own_rank = lax.dynamic_index_in_dim(rank_part, bt_position, 0, keepdims=False)
    own_slot = own_band * capacity + own_rank
    slot_range = jnp.arange(slot_count, dtype=jnp.int32)
    chooser = (own_slot[:, None] == slot_range[None, :]).astype(jnp.float32)
    outbound = jnp.einsum("xpqw,ws->xpqs", tile_stack, chooser, precision=highest)
    inbound = lax.all_to_all(outbound, "bt", split_axis=3, concat_axis=3, tiled=True)
    landed = band_part == bt_position
    slot_index = jnp.arange(bt_count, dtype=jnp.int32)[:, None] * capacity + rank_part
    slot_hits = ((slot_index[:, :, None] == slot_range[None, None, :]) & landed[:, :, None]).astype(
        jnp.float32
    )
    offset_table = tile_offset.reshape(bt_count, blocks)
    offset_part = lax.dynamic_slice_in_dim(offset_table, ch_position * per_band, per_band, 1)
    tile_range = jnp.arange(rows_band * cols_band, dtype=jnp.int32)
    tile_hits = (offset_part[:, :, None] == tile_range[None, None, :]).astype(jnp.float32)
    placing = jnp.einsum("iws,iwt->st", slot_hits, tile_hits, precision=highest)
    placed = jnp.einsum("xpqs,st->xpqt", inbound, placing, precision=highest)
    grid_block = placed.reshape(2, SUB, SUB, rows_band, cols_band).transpose(0, 3, 1, 4, 2)
    grid_block = grid_block.reshape(2, rows_band * SUB, cols_band * SUB)
    row_span = grid_block.shape[1]
    narrow = grid_block.shape[2] // bt_count
    sending = (
        grid_block.reshape(2, row_span, bt_count, narrow)
        .transpose(0, 2, 1, 3)
        .reshape(2, bt_count, row_span * narrow)
    )
    gathered = lax.all_to_all(sending, "bt", split_axis=1, concat_axis=1, tiled=True)
    along_rows = transform_rows(gathered.reshape(2, bt_count * row_span, narrow))
    spread = lax.all_to_all(
        lax.all_to_all(along_rows, "bt", split_axis=1, concat_axis=2, tiled=True),
        "ch",
        split_axis=1,
        concat_axis=2,
        tiled=True,
    )
    scale = 1.0 / (G1 * G2 * math.sqrt(TSLOT * CHANNELS))
    return transform_columns(spread) * scale


def solution(mesh):
    return jax.shard_map(
        shards,
        mesh=mesh,
        in_specs=(
            P(None, None, "ch", "bt"),
            P(None, None, "ch", "bt"),
            P(None, "ch", None),
            P("bt", None),
            P(),
            P(),
        ),
        out_specs=P(None, ("bt", "ch"), None),
        check_vma=False,
    )
```

profile of v0, /device:TPU:1, one launch (start us, length us, event | category | flops | bytes accessed | tf_op | source)
XLA Modules:
  0.0 395.1 jit_solution(15549429852581479042)
XLA Ops:
  2.7 1.8 reshape.178
  4.4 10.1 %all-to-all-start.1 = ((f32[8,1,2048]{2,1,0:T(1,128)}), f32[8,1,2048]{2,1,0:T(1,128)S(1)}, u32[]{:S(2)}, u32[]{:S(2)}) async-start(f32[8,1,2048]{2,1,0:T(1,128)} %reshape.178), calls=%async_computation.1 | async-start | bytes 131072 | tf_op jit(solution)/shard_map/all_to_all | solution.py:155
  15.2 1.7 reduce.5
  17.2 1.2 select_reduce_fusion
  18.4 1.3 copy.140
  19.8 1.8 reshape.180
  21.7 5.0 %all-to-all-start = ((f32[8,1,2048]{2,1,0:T(1,128)}), f32[8,1,2048]{2,1,0:T(1,128)S(1)}, u32[]{:S(2)}, u32[]{:S(2)}) async-start(f32[8,1,2048]{2,1,0:T(1,128)} %reshape.180), calls=%async_computation | async-start | bytes 131072 | tf_op jit(solution)/shard_map/all_to_all | solution.py:156
  27.9 1.2 reshape.179
  29.8 1.6 all-to-all-done
  32.1 1.2 reshape.181
  34.0 8.3 %fusion.3 = f32[32,32,32]{2,1,0:T(8,128)S(1)} fusion(f32[256,32]{0,1:T(8,128)S(1)} %copy.147, f32[256,32]{0,1:T(8,128)S(1)} %copy.146, f32[256,32]{0,1:T(8,128)S(1)} %copy.145, f32[256,32]{0,1:T(8,128)S(1)} %copy.142, f32[32]{0:T(128)S(1)} %fusion.191), kind=kOutput, calls=%fused_computation.7 | convolution fusion | flops 101974016 | bytes 262272 | tf_op jit(solution)/shard_map/klb,kmb->lmb/dot_general | solution.py:20
  42.3 8.5 %fusion.2 = f32[32,32,32]{2,1,0:T(8,128)S(1)} fusion(f32[256,32]{0,1:T(8,128)S(1)} %copy.147, f32[256,32]{0,1:T(8,128)S(1)} %copy.146, f32[256,32]{0,1:T(8,128)S(1)} %copy.145, f32[256,32]{0,1:T(8,128)S(1)} %copy.142, f32[32]{0:T(128)S(1)} %fusion.191), kind=kOutput, calls=%fused_computation.6 | convolution fusion | flops 101974016 | bytes 262272 | tf_op jit(solution)/shard_map/klb,kmb->lmb/dot_general | solution.py:23
  50.8 8.7 %fusion.15 = f32[32,32,32]{0,1,2:T(8,128)S(1)} fusion(f32[32,32,32]{2,1,0:T(8,128)S(1)} %fusion.3, f32[256,32]{0,1:T(8,128)S(1)} %copy.147, f32[256,32]{0,1:T(8,128)S(1)} %copy.146, f32[256,32]{0,1:T(8,128)S(1)} %copy.145, f32[256,32]{0,1:T(8,128)S(1)} %copy.142, f32[32]{0:T(128)S(1)} %fusion.191), kind=kOutput, calls=%fused_computation.18 | convolution fusion | flops 102006784 | bytes 393344 | tf_op jit(solution)/shard_map/klb,kmb->lmb/dot_general | solution.py:20
  59.8 8.5 %fusion.17 = f32[32,32,32]{0,1,2:T(8,128)S(1)} fusion(f32[32,32,32]{2,1,0:T(8,128)S(1)} %fusion.2, f32[256,32]{0,1:T(8,128)S(1)} %copy.147, f32[256,32]{0,1:T(8,128)S(1)} %copy.146, f32[256,32]{0,1:T(8,128)S(1)} %copy.145, f32[256,32]{0,1:T(8,128)S(1)} %copy.142, f32[32]{0:T(128)S(1)} %fusion.191), kind=kOutput, calls=%fused_computation.20 | convolution fusion | flops 102006784 | bytes 393344 | tf_op jit(solution)/shard_map/klb,kmb->lmb/dot_general | solution.py:23
  74.5 1.0 fusion.30
  75.5 4.4 %copy.159 = f32[2,32,32,128]{2,1,0,3:T(8,128)} copy(f32[2,32,32,128]{3,2,1,0:T(8,128)S(1)} %fusion.30) | data formatting | bytes 2097152 | tf_op jit(solution)/shard_map/xpqw,ws->xpqs/dot_general | solution.py:169
  80.0 4.7 %reshape.182 = f32[64,1,4096]{2,1,0:T(1,128)} reshape(f32[128,2,32,32]{3,2,1,0:T(8,128)} %bitcast.164) | data formatting | bytes 2097152
  84.7 14.3 %all-to-all-start.2 = ((f32[64,1,4096]{2,1,0:T(1,128)}), f32[64,1,4096]{2,1,0:T(1,128)S(1)}, u32[]{:S(2)}, u32[]{:S(2)}) async-start(f32[64,1,4096]{2,1,0:T(1,128)} %reshape.182), calls=%async_computation.2 | async-start | bytes 2097152 | tf_op jit(solution)/shard_map/all_to_all | solution.py:170
  99.2 1.3 convolution_bitcast_fusion
  100.5 50.0 %all-to-all-done.2 = f32[64,1,4096]{2,1,0:T(1,128)S(1)} async-done(((f32[64,1,4096]{2,1,0:T(1,128)}), f32[64,1,4096]{2,1,0:T(1,128)S(1)}, u32[]{:S(2)}, u32[]{:S(2)}) %all-to-all-start.2) | async-done | bytes 1048608 | tf_op jit(solution)/shard_map/all_to_all | solution.py:170
  150.5 3.2 reduce.8
  153.7 2.7 reshape.183
  156.4 10.6 %fusion = f32[2,32,32,128]{3,2,1,0:T(8,128)S(1)} fusion(f32[128,128,1,1]{1,0,3,2:T(8,128)S(1)} %convolution_bitcast_fusion, f32[2,32,32,128]{2,1,0,3:T(8,128)} %bitcast.165), kind=kOutput, calls=%fused_computation | convolution fusion | flops 402653184 | bytes 2162688 | tf_op jit(solution)/shard_map/xpqs,st->xpqt/dot_general | solution.py:181
  167.0 3.2 reshape.155
  170.2 6.4 %copy.162 = f32[2,32,32,4,32]{1,3,2,4,0:T(4,128)} copy(f32[2,32,32,4,32]{4,3,2,1,0:T(4,128)} %reshape.155) | data formatting | bytes 2097152 | tf_op jit(solution)/shard_map/reshape | solution.py:182
  176.6 3.7 reshape_reshape.4
  180.3 1.1 copy.163
  181.4 1.7 copy.164
  183.1 9.4 %all-to-all-start.3 = ((f32[2,64,2048]{2,0,1:T(2,128)}), f32[2,64,2048]{2,0,1:T(2,128)S(1)}, u32[]{:S(2)}, u32[]{:S(2)}) async-start(f32[2,64,2048]{2,0,1:T(2,128)} %copy.164), calls=%async_computation.3 | async-start | bytes 2097152 | tf_op jit(solution)/shard_map/all_to_all | solution.py:191
  192.7 50.7 %all-to-all-done.3 = f32[2,64,2048]{2,0,1:T(2,128)S(1)} async-done(((f32[2,64,2048]{2,0,1:T(2,128)}), f32[2,64,2048]{2,0,1:T(2,128)S(1)}, u32[]{:S(2)}, u32[]{:S(2)}) %all-to-all-start.3) | async-done | bytes 1048608 | tf_op jit(solution)/shard_map/all_to_all | solution.py:191
  243.4 1.6 fusion.266
  246.6 1.4 copy.167
  250.6 0.8 fusion.67
  251.4 0.8 fusion.66
  252.3 0.8 convolution_add_fusion.2
  253.8 0.8 convolution_subtract_fusion.2
  255.4 7.8 %copy.173 = f32[2,8192,16]{2,0,1:T(2,128)} copy(f32[2,8192,16]{1,2,0:T(8,128)S(1)} %pad_maximum_fusion) | data formatting | bytes 2097152 | tf_op jit(solution)/shard_map/stack | solution.py:26
  263.2 13.3 %reshape.184 = f32[64,1,4096]{2,1,0:T(1,128)S(1)} reshape(f32[8192,2,16]{2,1,0:T(2,128)} %bitcast.162) | data formatting | bytes 2097152
  276.6 58.0 %all_to_all.73 = f32[64,1,4096]{2,1,0:T(1,128)S(1)} all-to-all(f32[64,1,4096]{2,1,0:T(1,128)S(1)} %reshape.184), channel_id=1, replica_groups=mesh['bt'=64,'ch'=8] {'bt'}, dimensions={0} | all-to-all | bytes 2097152 | tf_op jit(solution)/shard_map/all_to_all | solution.py:194
  334.6 3.2 reduce.9
  337.8 12.6 %reshape.185 = f32[8192,2,16]{2,1,0:T(2,128)} reshape(f32[64,4096]{1,0:T(8,128)S(1)} %reduce.9) | data formatting | bytes 2097152
  350.4 9.2 %copy.186 = f32[2,64,128,16]{2,3,1,0:T(8,128)S(1)} copy(f32[2,64,128,16]{3,0,2,1:T(2,128)} %bitcast.163) | data formatting | bytes 2097152 | tf_op jit(solution)/shard_map/all_to_all | solution.py:194
  360.2 24.7 %all_to_all.74 = f32[2,128,1024]{2,0,1:T(2,128)S(1)} all-to-all(f32[2,128,1024]{2,0,1:T(2,128)S(1)} %copy.176), channel_id=1, replica_groups=mesh['bt'=64,'ch'=8] {'ch'}, dimensions={1} | all-to-all | bytes 2097152 | tf_op jit(solution)/shard_map/all_to_all | solution.py:193
  389.1 0.8 fusion.69
  389.9 0.8 fusion.68
  390.7 0.8 fusion.18
  392.3 0.8 fusion.19
  393.8 1.0 maximum_multiply_fusion
  (80 shorter events, 25.6 us)
Async XLA Ops:
  0.0 0.8 copy-start
  4.4 17.3 %all-to-all-start.1 = ((f32[8,1,2048]{2,1,0:T(1,128)}), f32[8,1,2048]{2,1,0:T(1,128)S(1)}, u32[]{:S(2)}, u32[]{:S(2)}) async-start(f32[8,1,2048]{2,1,0:T(1,128)} %reshape.178), calls=%async_computation.1 | async-start | bytes 131072 | tf_op jit(solution)/shard_map/all_to_all | solution.py:155
  21.7 9.7 %all-to-all-start = ((f32[8,1,2048]{2,1,0:T(1,128)}), f32[8,1,2048]{2,1,0:T(1,128)S(1)}, u32[]{:S(2)}, u32[]{:S(2)}) async-start(f32[8,1,2048]{2,1,0:T(1,128)} %reshape.180), calls=%async_computation | async-start | bytes 131072 | tf_op jit(solution)/shard_map/all_to_all | solution.py:156
  80.0 19.1 %copy-start.2 = (s32[16384]{0:T(1024)S(1)}, s32[16384]{0:T(1024)}, u32[]{:S(2)}) copy-start(s32[16384]{0:T(1024)} %param.11) | copy-start | bytes 196612
  84.7 65.8 %all-to-all-start.2 = ((f32[64,1,4096]{2,1,0:T(1,128)}), f32[64,1,4096]{2,1,0:T(1,128)S(1)}, u32[]{:S(2)}, u32[]{:S(2)}) async-start(f32[64,1,4096]{2,1,0:T(1,128)} %reshape.182), calls=%async_computation.2 | async-start | bytes 2097152 | tf_op jit(solution)/shard_map/all_to_all | solution.py:170
  183.1 60.3 %all-to-all-start.3 = ((f32[2,64,2048]{2,0,1:T(2,128)}), f32[2,64,2048]{2,0,1:T(2,128)S(1)}, u32[]{:S(2)}, u32[]{:S(2)}) async-start(f32[2,64,2048]{2,0,1:T(2,128)} %copy.164), calls=%async_computation.3 | async-start | bytes 2097152 | tf_op jit(solution)/shard_map/all_to_all | solution.py:191
  391.5 3.3 copy-start.1
where the time goes:
time: 400 us; the launch traced here: 395 us
  waiting for transfers between devices  102 us (26%)
  local copies, waits for them, and re-layouts  92.4 us (23%)
  blocking collectives  82.7 us (21%)
  matrix products  65 us (16%)
  starting transfers between devices  38.8 us (10%)
  other arithmetic  13.1 us (3%)
    all_to_all x1, blocking collectives, shards(): lax.all_to_all(along_rows, 'bt', split_axis=1, concat_axis=2, tiled=True)  58 us
    all_to_all x1, waiting for transfers between devices, shards(): lax.all_to_all(sending, 'bt', split_axis=1, concat_axis=1, tiled=True)  50.7 us
    all_to_all x1, waiting for transfers between devices, shards(): lax.all_to_all(outbound, 'bt', split_axis=3, concat_axis=3, tiled=True)  50 us
    unnamed x17, local copies, waits for them, and re-layouts  41.4 us
    all_to_all x1, blocking collectives, shards(): lax.all_to_all(lax.all_to_all(along_rows, 'bt', split_axis=1, concat_axis...  24.7 us
    all_to_all x1, starting transfers between devices, shards(): lax.all_to_all(outbound, 'bt', split_axis=3, concat_axis=3, tiled=True)  14.3 us
    dot_general x7, matrix products, complex_einsum(): jnp.einsum(form, left_side[1], right_side[1], precision=highest)  13.1 us
    dot_general x7, matrix products, complex_einsum(): jnp.einsum(form, left_side[1], right_side[0], precision=highest)  12.9 us
  transfers between devices with their start and end apart: 4, of which 3 were waited for; matrix products, arithmetic and copies ran while one was open for 3% of the time, Pallas kernels for 0%

commit v1 on v0

v1 whole, which is shorter than its diff:
```python
import math

import jax
import jax.numpy as jnp
import ml_dtypes
import numpy as np
from jax import lax
from jax.experimental import pallas as pl
from jax.experimental.pallas import tpu as pltpu
from jax.sharding import PartitionSpec as P

MESH = pl.DeviceIdType.MESH
NZ, NX, NCH = 16, 4, 8
SUB = 32
G = 8192
SPAN = G // NZ
BF = jnp.bfloat16
F32 = jnp.float32


def split_const(table):
    high = np.asarray(table, np.float32).astype(ml_dtypes.bfloat16)
    low = (np.asarray(table, np.float64) - high.astype(np.float64)).astype(np.float32).astype(ml_dtypes.bfloat16)
    return high, low


def taper_dft():
    pos = np.arange(SUB)
    x = (pos - SUB // 2) / SUB
    return np.exp(-2j * np.pi * np.outer(pos, x)) * (np.exp(-4.0 * x * x) / math.sqrt(SUB))[None, :]


def front_table():
    table = taper_dft()
    high, low = split_const(np.concatenate([table.real, table.imag], 0))
    return np.concatenate([high, high, low], 1)


def row_table():
    a = np.arange(G)
    u = np.exp(2j * np.pi * np.outer(a, np.arange(SUB)) / G) @ taper_dft()
    u = u.reshape(NZ, SPAN, SUB).transpose(0, 2, 1)
    w = np.concatenate(
        [np.concatenate([u.real, u.imag], 2), np.concatenate([-u.imag, u.real], 2)], 1
    )
    high, low = split_const(w)
    return np.concatenate([high, high, low, low], 1)


def row_phase():
    ang = 2 * np.pi * (np.outer(np.arange(256), np.arange(256)) % 256) / 256
    return np.concatenate([np.cos(ang), np.sin(ang)], 1).astype(np.float32)


def column_table():
    ang = 2 * np.pi * (np.outer(np.arange(256), np.arange(256)) % 256) / 256
    c, s = np.cos(ang), np.sin(ang)
    return split_const(np.concatenate([np.concatenate([c, s], 1), np.concatenate([-s, c], 1)], 0))


def column_twiddle():
    ang = 2 * np.pi * np.outer(np.arange(SUB), np.arange(256)) / G
    scale = 1.0 / (G * 16.0)
    return (np.concatenate([np.cos(ang), np.sin(ang)], 1) * scale).astype(np.float32)


def trig_coefficients():
    f = 0.5 * np.cos(np.pi * (np.arange(4000) + 0.5) / 4000)
    y = f * f
    cosine = np.polynomial.chebyshev.Chebyshev.fit(y, np.cos(2 * np.pi * f), 8, domain=[0, 0.25])
    sine = np.polynomial.chebyshev.Chebyshev.fit(
        y, np.sin(2 * np.pi * f) / f, 7, domain=[0, 0.25]
    )
    convert = np.polynomial.Polynomial
    return (
        [float(v) for v in cosine.convert(kind=convert).coef],
        [float(v) for v in sine.convert(kind=convert).coef],
    )


COS_C, SIN_C = trig_coefficients()


def horner(coefs, y):
    total = jnp.full_like(y, coefs[-1])
    for value in coefs[-2::-1]:
        total = total * y + value
    return total


def phasor(turns):
    f = turns - jnp.floor(turns + 0.5)
    y = f * f
    return horner(COS_C, y), f * horner(SIN_C, y)


def halves(v):
    high = v.astype(BF)
    return high, (v - high.astype(F32)).astype(BF)


def dot(a, b, dims=((1,), (0,))):
    return lax.dot_general(a, b, (dims, ((), ())), preferred_element_type=F32)


def lanes(shape):
    return lax.broadcasted_iota(jnp.int32, shape, 1)


def front_kernel(
    vis, off, gain, st, ttab, out,
    packed, landed, quant, image, tile,
    ch_send, ch_recv, x_send, x_recv, z_send, z_recv,
):
    bt, ch = lax.axis_index("bt"), lax.axis_index("ch")
    z, x = bt // NX, bt % NX
    ch_peer = [(bt, (ch + d) % NCH) for d in range(1, NCH)]
    x_peer = [(z * NX + (x + d) % NX, ch) for d in range(1, NX)]
    right = (((z + 1) % NZ) * NX + x, ch)
    left = (((z + NZ - 1) % NZ) * NX + x, ch)
    barrier = pltpu.get_barrier_semaphore()
    peers = ch_peer + x_peer + [right, left]
    for peer in peers:
        pl.semaphore_signal(barrier, inc=1, device_id=peer, device_id_type=MESH)

    g = gain[...]
    g0 = g.astype(BF)
    rest = g - g0.astype(F32)
    g1 = rest.astype(BF)
    g2 = (rest - g1.astype(F32)).astype(BF)
    parts = jnp.concatenate([g0, g1, g2], 0)
    stations = lax.broadcasted_iota(jnp.int32, (512, 256), 0)

    def pick(row):
        hot = jnp.where(stations == st[row : row + 1, :], 1.0, 0.0).astype(BF)
        got = dot(parts, hot)
        got = (got[0:16] + got[16:32]) + got[32:48]
        return got[0:8], got[8:16]

    pr, pi = pick(0)
    qr, qi = pick(1)
    ar = pr * qr + pi * qi
    ai = pi * qr - pr * qi
    rows_r, rows_i, rows_u, rows_v = [], [], [], []
    for t in range(4):
        vr, vi = vis[0, t], vis[1, t]
        rows_r.append(vr * ar - vi * ai)
        rows_i.append(vr * ai + vi * ar)
        rows_u.append(off[0, t])
        rows_v.append(off[1, t])
    packed[...] = jnp.concatenate(rows_r + rows_i + rows_u + rows_v, 0).T
    landed[ch] = packed[pl.ds(pl.multiple_of(ch * 32, 32), 32), :]

    pl.semaphore_wait(barrier, len(peers))
    copies = []
    for d, peer in enumerate(ch_peer):
        copy = pltpu.make_async_remote_copy(
            src_ref=packed.at[pl.ds(pl.multiple_of(peer[1] * 32, 32), 32)],
            dst_ref=landed.at[ch],
            send_sem=ch_send.at[d],
            recv_sem=ch_recv.at[d],
            device_id=peer,
            device_id_type=MESH,
        )
        copy.start()
        copies.append(copy)
    for copy in copies:
        copy.wait()

    lane = lanes((32, 128))
    for h in range(2):
        for q in range(4):
            got = None
            for i in range(4):
                shift = (32 * (i - q)) % 128
                piece = landed[4 * h + i]
                if shift:
                    piece = pltpu.roll(piece, shift, 1)
                got = piece if got is None else jnp.where(lane >= 32 * i, piece, got)
            quant[q, :, 128 * h : 128 * h + 128] = got

    xl = (lax.broadcasted_iota(jnp.int32, (32, 256), 0) - 16).astype(F32) * (1.0 / 32.0)
    sign = jnp.where((lane // 32) % 2 == 0, -1.0, 1.0)

    def one_block(b):
        wr = quant[0, pl.ds(b, 1), :]
        wi = quant[1, pl.ds(b, 1), :]
        u = quant[2, pl.ds(b, 1), :]
        v = quant[3, pl.ds(b, 1), :]
        cu, su = phasor(xl * u)
        rr, ri = phasor(xl * v)
        lr = wr * cu - wi * su
        li = wr * su + wi * cu
        lrh, lrl = halves(lr)
        lih, lil = halves(li)
        rrh, rrl = halves(rr)
        rih, ril = halves(ri)
        d = dot(
            jnp.concatenate([rrh, rih, rrl, ril], 0),
            jnp.concatenate([lrh, lih, lrl, lil], 0),
            ((1,), (1,)),
        )
        pr_ = d[0:32] + d[64:96]
        pi_ = d[32:64] + d[96:128]
        pr_ = pr_ + pltpu.roll(pr_, 64, 1)
        pi_ = pi_ + pltpu.roll(pi_, 64, 1)
        return pr_ + sign * pltpu.roll(pi_, 32, 1)

    def pair(p, carry):
        both = jnp.where(lane < 64, one_block(2 * p), one_block(2 * p + 1))
        image[:, pl.ds(pl.multiple_of(p * 128, 128), 128)] = both
        return carry

    lax.fori_loop(0, 16, pair, 0)

    def to_tile(p, carry):
        at = pl.ds(pl.multiple_of(p * 256, 256), 256)
        high, low = halves(image[:, at])
        ts = dot(ttab[...], jnp.concatenate([high, low, high], 0))
        for k in range(2):
            tr = ts[0:32, 128 * k : 128 * k + 128]
            ti = ts[32:64, 128 * k : 128 * k + 128]
            other = jnp.where(sign < 0, pltpu.roll(ti, 96, 1), pltpu.roll(ti, 32, 1))
            tile[:, pl.ds(pl.multiple_of(p * 256 + 128 * k, 128), 128)] = tr + sign * other
        return carry

    lax.fori_loop(0, 8, to_tile, 0)

    copies = []
    for d, peer in enumerate(x_peer):
        to = (x + d + 1) % NX
        copy = pltpu.make_async_remote_copy(
            src_ref=tile.at[pl.ds(pl.multiple_of(to * 8, 8), 8)],
            dst_ref=out.at[z, x],
            send_sem=x_send.at[d],
            recv_sem=x_recv.at[d],
            device_id=peer,
            device_id_type=MESH,
        )
        copy.start()
        copies.append(copy)
    out[z, x] = tile[pl.ds(pl.multiple_of(x * 8, 8), 8), :]
    for copy in copies:
        copy.wait()

    last = NZ // 2 - 1
    sent = {}

    def hop(way, step, part):
        slot = (z + NZ - step) % NZ if way == 0 else (z + step) % NZ
        copy = pltpu.make_async_remote_copy(
            src_ref=out.at[slot, part],
            dst_ref=out.at[slot, part],
            send_sem=z_send.at[way, step, part],
            recv_sem=z_recv.at[way, step, part],
            device_id=right if way == 0 else left,
            device_id_type=MESH,
        )
        copy.start()
        sent[way, step, part] = copy

    for step in range(NZ // 2):
        for part in range(NX):
            for way in range(2):
                if step:
                    sent[way, step - 1, part].wait_recv()
                if step < last or (part < NX // 2) == (way == 0):
                    hop(way, step, part)
    for (way, step, part), copy in sent.items():
        if step == last:
            copy.wait_recv()
    for copy in sent.values():
        copy.wait_send()


def front(vis, off, gain, st):
    vmem = pl.BlockSpec(memory_space=pltpu.VMEM)
    dma = pltpu.SemaphoreType.DMA
    return pl.pallas_call(
        front_kernel,
        out_shape=jax.ShapeDtypeStruct((NZ, NX, 8, 2048), F32),
        in_specs=[vmem] * 5,
        out_specs=vmem,
        scratch_shapes=[
            pltpu.VMEM((256, 128), F32),
            pltpu.VMEM((8, 32, 128), F32),
            pltpu.VMEM((4, 32, 256), F32),
            pltpu.VMEM((32, 2048), F32),
            pltpu.VMEM((32, 2048), F32),
            dma((NCH - 1,)),
            dma((NCH - 1,)),
            dma((NX - 1,)),
            dma((NX - 1,)),
            dma((2, NZ // 2, NX)),
            dma((2, NZ // 2, NX)),
        ],
        compiler_params=pltpu.CompilerParams(
            collective_id=0, has_side_effects=True, vmem_limit_bytes=40 << 20
        ),
    )(vis, off, gain, st, jnp.asarray(front_table()))


def rows_kernel(places, zat, tiles, wtab, phase, out, lhs, prod, acc):
    step = pl.program_id(0)

    @pl.when(step == 0)
    def _():
        acc[...] = jnp.zeros_like(acc)

    lane = lanes((8, 128))
    low_half = lane < 64

    def one_source(xs, carry):
        for p in range(16):
            v = tiles[0, xs, :, 128 * p : 128 * p + 128]
            high = v.astype(BF).astype(F32)
            rolled = pltpu.roll(v - high, 64, 1)
            first = jnp.concatenate(
                [jnp.where(low_half, high, rolled), jnp.where(low_half, high, 0.0)], 1
            )
            second = jnp.concatenate(
                [jnp.where(low_half, rolled, high), jnp.where(low_half, 0.0, high)], 1
            )
            lhs[16 * p : 16 * p + 16, :] = jnp.concatenate([first, second], 0).astype(BF)
        prod[...] = dot(lhs[...], wtab[0])

        def one_tile(b, carry):
            place = places[(step * NX + xs) * 32 + b]
            tr, tc = place // 32, place % 32
            c = phase[pl.ds(tr, 1), 0:256]
            s = phase[pl.ds(tr, 1), 256:512]
            rows = pl.ds(pl.multiple_of(b * 8, 8), 8)
            for h in range(2):
                re, im = slice(256 * h, 256 * h + 256), slice(512 + 256 * h, 768 + 256 * h)
                pr, pi = prod[rows, re], prod[rows, im]
                acc[tc, :, re] += c * pr - s * pi
                acc[tc, :, im] += c * pi + s * pr
            return carry

        lax.fori_loop(0, 32, one_tile, 0, unroll=4)
        return carry

    lax.fori_loop(0, NX, one_source, 0)

    @pl.when(step == NZ - 1)
    def _():
        for q in range(8):
            prod[32 * q : 32 * q + 32, :] = acc[:, q, :]
        for k in range(8):
            out[128 * k : 128 * k + 128, :] = prod[:, 128 * k : 128 * k + 128].T


def image_rows(places, zat, tiles):
    return pl.pallas_call(
        rows_kernel,
        out_shape=jax.ShapeDtypeStruct((1024, 256), F32),
        grid_spec=pltpu.PrefetchScalarGridSpec(
            num_scalar_prefetch=2,
            grid=(NZ,),
            in_specs=[
                pl.BlockSpec((1, NX, 8, 2048), lambda i, p, z: (i, 0, 0, 0)),
                pl.BlockSpec((1, 256, 1024), lambda i, p, z: (z[0], 0, 0)),
                pl.BlockSpec((256, 512), lambda i, p, z: (0, 0)),
            ],
            out_specs=pl.BlockSpec((1024, 256), lambda i, p, z: (0, 0)),
            scratch_shapes=[
                pltpu.VMEM((256, 256), BF),
                pltpu.VMEM((256, 1024), F32),
                pltpu.VMEM((32, 8, 1024), F32),
            ],
        ),
        compiler_params=pltpu.CompilerParams(vmem_limit_bytes=40 << 20),
    )(places, zat, tiles, jnp.asarray(row_table()), jnp.asarray(row_phase()))


def spread_kernel(rows, out, local, send, recv):
    bt, ch = lax.axis_index("bt"), lax.axis_index("ch")
    z, x = bt // NX, bt % NX
    me = x * NCH + ch
    n = NX * NCH
    barrier = pltpu.get_barrier_semaphore()
    ids = [(me + d) % n for d in range(1, n)]
    peers = [(z * NX + i // NCH, i % NCH) for i in ids]
    for peer in peers:
        pl.semaphore_signal(barrier, inc=1, device_id=peer, device_id_type=MESH)
    own = pltpu.make_async_copy(rows.at[:, me], out.at[me], local)
    own.start()
    pl.semaphore_wait(barrier, n - 1)
    copies = []
    for d, (i, peer) in enumerate(zip(ids, peers)):
        copy = pltpu.make_async_remote_copy(
            src_ref=rows.at[:, i],
            dst_ref=out.at[me],
            send_sem=send.at[d],
            recv_sem=recv.at[d],
            device_id=peer,
            device_id_type=MESH,
        )
        copy.start()
        copies.append(copy)
    for copy in copies:
        copy.wait()
    own.wait()


def spread(rows):
    vmem = pl.BlockSpec(memory_space=pltpu.VMEM)
    n = NX * NCH
    return pl.pallas_call(
        spread_kernel,
        out_shape=jax.ShapeDtypeStruct((n, 2, 16, 256), F32),
        in_specs=[vmem],
        out_specs=vmem,
        scratch_shapes=[
            pltpu.SemaphoreType.DMA,
            pltpu.SemaphoreType.DMA((n - 1,)),
            pltpu.SemaphoreType.DMA((n - 1,)),
        ],
        compiler_params=pltpu.CompilerParams(
            collective_id=1, has_side_effects=True, vmem_limit_bytes=40 << 20
        ),
    )(rows)


def turn(values):
    n = len(values)
    if n == 1:
        return values
    even, odd = turn(values[0::2]), turn(values[1::2])
    low, high = [], []
    for k in range(n // 2):
        er, ei = even[k]
        xr, xi = odd[k]
        if k == 0:
            tr, ti = xr, xi
        elif 4 * k == n:
            tr, ti = -xi, xr
        else:
            c, s = math.cos(2 * math.pi * k / n), math.sin(2 * math.pi * k / n)
            tr, ti = c * xr - s * xi, c * xi + s * xr
        low.append((er + tr, ei + ti))
        high.append((er - tr, ei - ti))
    return low + high


def columns_kernel(parts, whigh, wlow, twiddle, out, vhigh, vlow, mid):
    lane = lanes((16, 128))

    def one_x(x, carry):
        for r in range(2):
            for h in range(2):
                for j in range(2):
                    pieces = [parts[x * 8 + 4 * h + i, r, :, 128 * j : 128 * j + 128] for i in range(4)]
                    for jj in range(4):
                        got = None
                        for i in range(4):
                            shift = (32 * (i - jj)) % 128
                            piece = pltpu.roll(pieces[i], shift, 1) if shift else pieces[i]
                            got = piece if got is None else jnp.where(lane >= 32 * i, piece, got)
                        high, low = halves(got)
                        rows = pl.ds(pl.multiple_of((x * 8 + 4 * j + jj) * 16, 16), 16)
                        at = slice(256 * r + 128 * h, 256 * r + 128 * h + 128)
                        vhigh[rows, at] = high
                        vlow[rows, at] = low
        return carry

    lax.fori_loop(0, NX, one_x, 0)
    mid[...] = dot(vhigh[...], whigh[...]) + (dot(vlow[...], whigh[...]) + dot(vhigh[...], wlow[...]))
    for a in range(2):
        for e in range(2):
            values = []
            for q in range(SUB):
                rows = slice(16 * q + 8 * a, 16 * q + 8 * a + 8)
                zr = mid[rows, 128 * e : 128 * e + 128]
                zi = mid[rows, 256 + 128 * e : 384 + 128 * e]
                c = twiddle[q : q + 1, 128 * e : 128 * e + 128]
                s = twiddle[q : q + 1, 256 + 128 * e : 384 + 128 * e]
                values.append((c * zr - s * zi, c * zi + s * zr))
            for k, (re, im) in enumerate(turn(values)):
                at = slice(256 * k + 128 * e, 256 * k + 128 * e + 128)
                out[0, 8 * a : 8 * a + 8, at] = re
                out[1, 8 * a : 8 * a + 8, at] = im


def columns(parts):
    vmem = pl.BlockSpec(memory_space=pltpu.VMEM)
    high, low = column_table()
    return pl.pallas_call(
        columns_kernel,
        out_shape=jax.ShapeDtypeStruct((2, 16, G), F32),
        in_specs=[vmem] * 4,
        out_specs=vmem,
        scratch_shapes=[
            pltpu.VMEM((512, 512), BF),
            pltpu.VMEM((512, 512), BF),
            pltpu.VMEM((512, 512), F32),
        ],
        compiler_params=pltpu.CompilerParams(vmem_limit_bytes=40 << 20),
    )(parts, jnp.asarray(high), jnp.asarray(low), jnp.asarray(column_twiddle()))


def shards(visibility, cell_offset, station_gain, stations, row_band, tile_offset):
    ch = lax.axis_index("ch")
    zat = (lax.axis_index("bt") // NX).astype(jnp.int32).reshape(1)
    place = (row_band.reshape(-1) * 128 + tile_offset).reshape(NZ * NX, NCH, 32)
    place = lax.dynamic_index_in_dim(place, ch, 1, keepdims=False).reshape(-1)
    tiles = front(visibility, cell_offset, station_gain.reshape(16, 512), stations.T)
    rows = image_rows(place, zat, tiles)
    parts = spread(rows.reshape(2, NX * NCH, 16, 256))
    return columns(parts)


def solution(mesh):
    return jax.shard_map(
        shards,
        mesh=mesh,
        in_specs=(
            P(None, None, "ch", "bt"),
            P(None, None, "ch", "bt"),
            P(None, "ch", None),
            P("bt", None),
            P(),
            P(),
        ),
        out_specs=P(None, ("bt", "ch"), None),
        check_vma=False,
    )
```

time: 400 us -> 160 us (0.40); the launches traced: 395 us -> 159 us
  Pallas kernels: 0 us -> 149 us
  waiting for transfers between devices: 102 us -> 0 us
  local copies, waits for them, and re-layouts: 92.4 us -> 8.55 us
  blocking collectives: 82.7 us -> 0 us
  matrix products: 65 us -> 0 us
  starting transfers between devices: 38.8 us -> 0 us
  other arithmetic: 13.1 us -> 1.75 us
    pallas_call x0 -> x4, Pallas kernels: none -> 149 us  [the longest x1 77.1 us: front(): pl.pallas_call(front_kernel, out_shape=jax.ShapeDtypeStruct((NZ, NX, 8, 2...]
    all_to_all x4 -> x0, waiting for transfers between devices: 102 us -> none  [the longest x1 50.7 us: shards(): lax.all_to_all(sending, 'bt', split_axis=1, concat_axis=1, tiled=True)]
    all_to_all x2 -> x0, blocking collectives: 82.7 us -> none  [the longest x1 58 us: shards(): lax.all_to_all(along_rows, 'bt', split_axis=1, concat_axis=2, tiled=True)]
    dot_general x33 -> x0, matrix products: 65 us -> none  [the longest x7 13.1 us: complex_einsum(): jnp.einsum(form, left_side[1], right_side[1], precision=highest)]
    all_to_all x4 -> x0, starting transfers between devices: 38.8 us -> none  [the longest x1 14.3 us: shards(): lax.all_to_all(outbound, 'bt', split_axis=3, concat_axis=3, tiled=True)]
    unnamed x17 -> x20, local copies, waits for them, and re-layouts: 41.4 us -> 8.27 us
    another operation x7 -> x0, local copies, waits for them, and re-layouts: 13.5 us -> none  [the longest x5 9.25 us: complex_einsum(): return jnp.stack([real_part, imag_part])]
    all_to_all x6 -> x0, local copies, waits for them, and re-layouts: 11.6 us -> none  [the longest x2 9.8 us: shards(): lax.all_to_all(along_rows, 'bt', split_axis=1, concat_axis=2, tiled=True)]
  transfers between devices with their start and end apart: 4 -> 0, of which waited for: 3 -> 0; matrix products, arithmetic and copies ran while one was open for 3% -> 0% of each run, Pallas kernels for 0% -> 0%
where the time goes in v1:
time: 160 us; the launch traced here: 159 us
  Pallas kernels  149 us (93%)
  local copies, waits for them, and re-layouts  8.55 us (5%)
  other arithmetic  1.75 us (1%)
    pallas_call x1, Pallas kernels, front(): pl.pallas_call(front_kernel, out_shape=jax.ShapeDtypeStruct((NZ, NX, 8, 2...  77.1 us
    pallas_call x1, Pallas kernels, image_rows(): pl.pallas_call(rows_kernel, out_shape=jax.ShapeDtypeStruct((1024, 256), F...  46.6 us
    pallas_call x1, Pallas kernels, spread(): pl.pallas_call(spread_kernel, out_shape=jax.ShapeDtypeStruct((n, 2, 16, 2...  21.8 us
    unnamed x20, local copies, waits for them, and re-layouts  8.27 us
    pallas_call x1, Pallas kernels, columns(): pl.pallas_call(columns_kernel, out_shape=jax.ShapeDtypeStruct((2, 16, G),...  3.33 us

profile of v1, /device:TPU:1, one launch (start us, length us, event | category | flops | bytes accessed | tf_op | source)
XLA Modules:
  0.0 159.3 jit_solution(4063155513973434262)
XLA Ops:
  0.0 0.9 broadcast_multiply_fusion
  0.9 0.9 add.8
  1.8 0.1 reshape.19
  1.9 0.1 dynamic-slice_reduce_fusion
  2.0 0.1 reshape.20.places
  2.1 0.0 copy-start.4
  2.1 0.8 copy-done.4
  2.9 0.0 copy-start.5
  2.9 0.8 copy-done.5
  3.7 0.0 copy-start.7
  3.7 0.8 copy-done.7
  4.5 0.0 copy-start.8
  4.5 0.7 copy-done.8
  5.2 0.0 copy-start.9
  5.2 0.7 copy-done.9
  5.9 77.1 %shard_map.118.tiles = f32[16,4,8,2048]{3,2,1,0:T(8,128)S(1)} custom-call(f32[2,4,8,256]{3,2,1,0:T(8,128)S(1)} %copy-done.4, f32[2,4,8,256]{3,2,1,0:T(8,128)S(1)} %copy-done.5, f32[16,512]{1,0:T(8,128)S(1)} %bitcast.6, s32[2,256]{1,0:T(2,128)S(1)} %bitcast.7, bf16[64,96]{1,0:T(8,128)(2,1)S(1)} %copy-done.8), custom_call_target="tpu_custom_call" | custom-call | tf_op jit(solution)/shard_map/pallas_call | solution.py:279
  83.0 0.0 copy-start
  83.0 3.4 %copy-done = bf16[16,256,1024]{2,1,0:T(8,128)(2,1)S(1)} copy-done((bf16[16,256,1024]{2,1,0:T(8,128)(2,1)S(1)}, bf16[16,256,1024]{2,1,0:T(8,128)(2,1)}, u32[]{:S(2)}) %copy-start) | copy-done | bytes 8388632
  86.4 0.0 copy-start.3
  86.4 1.0 copy-done.3
  87.4 0.0 copy-start.1
  87.4 0.0 copy-start.2
  87.4 0.0 copy-start.6
  87.4 46.6 %shard_map.119 = f32[1024,256]{1,0:T(8,128)S(1)} custom-call(s32[2048]{0:T(1024)S(1)} %reshape.20.places, s32[1]{0:T(128)} %bitcast.1.zat, f32[16,4,8,2048]{3,2,1,0:T(8,128)S(1)} %shard_map.118.tiles, bf16[16,256,1024]{2,1,0:T(8,128)(2,1)S(1)} %copy-done, f32[256,512]{1,0:T(8,128)S(1)} %copy-done.3), custom_call_target="tpu_custom_call" | custom-call | tf_op jit(solution)/shard_map/pallas_call | solution.py:354
  134.1 21.8 %shard_map.120.parts = f32[32,2,16,256]{3,2,1,0:T(8,128)S(1)} custom-call(f32[2,32,16,256]{3,2,1,0:T(8,128)S(1)} %bitcast.5), custom_call_target="tpu_custom_call" | custom-call | tf_op jit(solution)/shard_map/pallas_call | solution.py:409
  155.9 0.0 copy-done.1
  155.9 0.0 copy-done.2
  156.0 0.0 copy-done.6
  156.0 3.3 %shard_map.121 = f32[2,16,8192]{2,1,0:T(8,128)} custom-call(f32[32,2,16,256]{3,2,1,0:T(8,128)S(1)} %shard_map.120.parts, bf16[512,512]{1,0:T(8,128)(2,1)S(1)} %copy-done.2, bf16[512,512]{1,0:T(8,128)(2,1)S(1)} %copy-done.1, f32[32,512]{1,0:T(8,128)S(1)} %copy-done.6), custom_call_target="tpu_custom_call" | custom-call | tf_op jit(solution)/shard_map/pallas_call | solution.py:488
Async XLA Ops:
  2.1 0.8 copy-start.4
  2.9 0.8 copy-start.5
  3.7 0.8 copy-start.7
  4.5 0.7 copy-start.8
  5.2 0.7 copy-start.9
  83.0 3.4 %copy-start = (bf16[16,256,1024]{2,1,0:T(8,128)(2,1)S(1)}, bf16[16,256,1024]{2,1,0:T(8,128)(2,1)}, u32[]{:S(2)}) copy-start(bf16[16,256,1024]{2,1,0:T(8,128)(2,1)} %constant.45.clone.wtab) | copy-start | bytes 25165828
  86.4 1.0 copy-start.3
  87.4 68.5 %copy-start.1 = (bf16[512,512]{1,0:T(8,128)(2,1)S(1)}, bf16[512,512]{1,0:T(8,128)(2,1)}, u32[]{:S(2)}) copy-start(bf16[512,512]{1,0:T(8,128)(2,1)} %constant.48.clone.wlow) | copy-start | bytes 1572868
  87.4 68.5 %copy-start.2 = (bf16[512,512]{1,0:T(8,128)(2,1)S(1)}, bf16[512,512]{1,0:T(8,128)(2,1)}, u32[]{:S(2)}) copy-start(bf16[512,512]{1,0:T(8,128)(2,1)} %constant.47.clone.whigh) | copy-start | bytes 1572868
  87.4 68.5 %copy-start.6 = (f32[32,512]{1,0:T(8,128)S(1)}, f32[32,512]{1,0:T(8,128)}, u32[]{:S(2)}) copy-start(f32[32,512]{1,0:T(8,128)} %constant.49.clone.twiddle) | copy-start | bytes 196612

commit v2 on v1

v2 whole, which is shorter than its diff:
```python
import math

import jax
import jax.numpy as jnp
import numpy as np
from jax import lax
from jax.experimental import pallas as pl
from jax.experimental.pallas import tpu as pltpu
from jax.sharding import PartitionSpec as P

MESH = pl.DeviceIdType.MESH
NZ, NX, NCH = 16, 4, 8
SUB = 32
G = 8192
SPAN = G // NZ
BF = jnp.bfloat16
F32 = jnp.float32


def taper_dft():
    half = SUB // 2
    pos = np.concatenate([np.arange(half, SUB), [0], np.arange(half - 1, 0, -1)])
    x = (pos - half) / SUB
    return np.exp(-2j * np.pi * np.outer(np.arange(SUB), x)) * (np.exp(-4.0 * x * x) / math.sqrt(SUB))[None, :]


def front_table():
    table = taper_dft()
    return np.concatenate([table.real, table.imag], 0).astype(np.float32)


def row_table():
    a = np.arange(G)
    u = np.exp(2j * np.pi * np.outer(a, np.arange(SUB)) / G) @ taper_dft()
    u = u.reshape(NZ, SPAN, SUB).transpose(0, 2, 1)
    w = np.concatenate(
        [np.concatenate([u.real, u.imag], 2), np.concatenate([-u.imag, u.real], 2)], 1
    )
    return w.astype(np.float32)


def column_table():
    ang = 2 * np.pi * (np.outer(np.arange(256), np.arange(256)) % 256) / 256
    return np.concatenate([np.cos(ang), np.sin(ang)], 1).astype(np.float32)


def column_twiddle():
    ang = 2 * np.pi * np.outer(np.arange(SUB), np.arange(256)) / G
    scale = 1.0 / (G * 16.0)
    return (np.concatenate([np.cos(ang), np.sin(ang)], 1) * scale).astype(np.float32)


def trig_coefficients():
    f = 0.5 * np.cos(np.pi * (np.arange(4000) + 0.5) / 4000)
    y = f * f
    cosine = np.polynomial.chebyshev.Chebyshev.fit(y, np.cos(2 * np.pi * f), 7, domain=[0, 0.25])
    sine = np.polynomial.chebyshev.Chebyshev.fit(
        y, np.sin(2 * np.pi * f) / f, 6, domain=[0, 0.25]
    )
    convert = np.polynomial.Polynomial
    return (
        [float(v) for v in cosine.convert(kind=convert).coef],
        [float(v) for v in sine.convert(kind=convert).coef],
    )


COS_C, SIN_C = trig_coefficients()


def horner(coefs, y):
    total = jnp.full_like(y, coefs[-1])
    for value in coefs[-2::-1]:
        total = total * y + value
    return total


def phasor(turns):
    f = turns - jnp.floor(turns + 0.5)
    y = f * f
    return horner(COS_C, y), f * horner(SIN_C, y)


def steps(row, u):
    c, s = phasor(row * u)
    end_c = c[8:9] * c[8:9] - s[8:9] * s[8:9]
    end_s = -2.0 * c[8:9] * s[8:9]
    first = lax.broadcasted_iota(jnp.int32, c.shape, 0) == 0
    return (
        jnp.concatenate([c, jnp.where(first, end_c, c)], 0),
        jnp.concatenate([s, jnp.where(first, end_s, -s)], 0),
    )


def halves(v):
    high = v.astype(BF)
    return high, (v - high.astype(F32)).astype(BF)


def dot(a, b, dims=((1,), (0,))):
    return lax.dot_general(a, b, (dims, ((), ())), preferred_element_type=F32)


def lanes(shape):
    return lax.broadcasted_iota(jnp.int32, shape, 1)


def front_kernel(
    vis_hbm, off_hbm, gain_hbm, st_hbm, band_hbm, place_hbm, ttab_hbm, tiles, where_out,
    vis, off, gain, st, band, place, ttab,
    packed, landed, quant, image, tile,
    load, keep, ch_send, ch_recv, x_send, x_recv, z_send, z_recv,
):
    bt, ch = lax.axis_index("bt"), lax.axis_index("ch")
    z, x = bt // NX, bt % NX
    ch_peer = [(bt, (ch + d) % NCH) for d in range(1, NCH)]
    x_peer = [(z * NX + (x + d) % NX, ch) for d in range(1, NX)]
    right = (((z + 1) % NZ) * NX + x, ch)
    left = (((z + NZ - 1) % NZ) * NX + x, ch)
    barrier = pltpu.get_barrier_semaphore()
    peers = ch_peer + x_peer + [right, left]
    for peer in peers:
        pl.semaphore_signal(barrier, inc=1, device_id=peer, device_id_type=MESH)
    loads = [
        pltpu.make_async_copy(src, dst, load.at[i])
        for i, (src, dst) in enumerate(
            [
                (gain_hbm, gain), (st_hbm, st), (vis_hbm, vis), (off_hbm, off), (band_hbm, band),
                (place_hbm, place), (ttab_hbm, ttab),
            ]
        )
    ]
    for copy in loads:
        copy.start()

    loads[0].wait()
    loads[1].wait()
    g = gain[...]
    g0 = g.astype(BF)
    rest = g - g0.astype(F32)
    g1 = rest.astype(BF)
    g2 = (rest - g1.astype(F32)).astype(BF)
    parts = jnp.concatenate([g0, g1, g2], 0)
    stations = lax.broadcasted_iota(jnp.int32, (512, 256), 0)

    def pick(row):
        hot = jnp.where(stations == st[row : row + 1, :], 1.0, 0.0).astype(BF)
        got = dot(parts, hot)
        got = (got[0:16] + got[16:32]) + got[32:48]
        return got[0:8], got[8:16]

    pr, pi = pick(0)
    qr, qi = pick(1)
    ar = pr * qr + pi * qi
    ai = pi * qr - pr * qi
    loads[2].wait()
    loads[3].wait()
    rows_r, rows_i, rows_u, rows_v = [], [], [], []
    for t in range(4):
        vr, vi = vis[0, t], vis[1, t]
        rows_r.append(vr * ar - vi * ai)
        rows_i.append(vr * ai + vi * ar)
        rows_u.append(off[0, t])
        rows_v.append(off[1, t])
    packed[...] = jnp.concatenate(rows_r + rows_i + rows_u + rows_v, 0).T

    pl.semaphore_wait(barrier, len(peers))
    copies = []
    for d, peer in enumerate(ch_peer):
        copy = pltpu.make_async_remote_copy(
            src_ref=packed.at[pl.ds(pl.multiple_of(peer[1] * 32, 32), 32)],
            dst_ref=landed.at[ch],
            send_sem=ch_send.at[d],
            recv_sem=ch_recv.at[d],
            device_id=peer,
            device_id_type=MESH,
        )
        copy.start()
        copies.append(copy)
    landed[ch] = packed[pl.ds(pl.multiple_of(ch * 32, 32), 32), :]

    for copy in loads[4:7]:
        copy.wait()
    lane16 = lanes((NZ, 128))
    where = None
    for xs in range(NX):
        at = pl.ds(2 * xs + ch // 4, NZ, stride=8)
        piece = band[at, :] * 128 + place[at, :]
        piece = pltpu.roll(piece, (32 * xs + 128 - 32 * (ch % 4)) % 128, 1)
        where = piece if where is None else jnp.where(lane16 >= 32 * xs, piece, where)
    where_out[...] = where
    for copy in copies:
        copy.wait()

    lane = lanes((32, 128))
    for h in range(2):
        for q in range(4):
            got = None
            for i in range(4):
                shift = (32 * (i - q)) % 128
                piece = landed[4 * h + i]
                if shift:
                    piece = pltpu.roll(piece, shift, 1)
                got = piece if got is None else jnp.where(lane >= 32 * i, piece, got)
            quant[q, :, 128 * h : 128 * h + 128] = got

    xl = lax.broadcasted_iota(jnp.int32, (16, 256), 0).astype(F32) * (1.0 / 32.0)
    sign = jnp.where((lane // 32) % 2 == 0, -1.0, 1.0)

    def one_block(b):
        wr = quant[0, pl.ds(b, 1), :]
        wi = quant[1, pl.ds(b, 1), :]
        u = quant[2, pl.ds(b, 1), :]
        v = quant[3, pl.ds(b, 1), :]
        cu, su = steps(xl, u)
        rr, ri = steps(xl, v)
        lr = wr * cu - wi * su
        li = wr * su + wi * cu
        lrh, lrl = halves(lr)
        lih, lil = halves(li)
        rrh, rrl = halves(rr)
        rih, ril = halves(ri)
        d = dot(
            jnp.concatenate([rrh, rih, rrl, ril], 0),
            jnp.concatenate([lrh, lih, lrl, lil], 0),
            ((1,), (1,)),
        )
        pr_ = d[0:32] + d[64:96]
        pi_ = d[32:64] + d[96:128]
        pr_ = pr_ + pltpu.roll(pr_, 64, 1)
        pi_ = pi_ + pltpu.roll(pi_, 64, 1)
        return pr_ + sign * pltpu.roll(pi_, 32, 1)

    def x_copy(c, d):
        to = (x + d + 1) % NX
        return pltpu.make_async_remote_copy(
            src_ref=tile.at[c, pl.ds(pl.multiple_of(to * 8, 8), 8)],
            dst_ref=tiles.at[z, c, x],
            send_sem=x_send.at[c, d],
            recv_sem=x_recv.at[c, d],
            device_id=x_peer[d],
            device_id_type=MESH,
        )

    sent = {}

    def hop(way, step, c):
        slot = (z + NZ - step) % NZ if way == 0 else (z + step) % NZ
        copy = pltpu.make_async_remote_copy(
            src_ref=tiles.at[slot, c],
            dst_ref=tiles.at[slot, c],
            send_sem=z_send.at[way, step, c],
            recv_sem=z_recv.at[way, step, c],
            device_id=right if way == 0 else left,
            device_id_type=MESH,
        )
        copy.start()
        sent[way, step, c] = copy

    thigh, tlow = halves(ttab[...])
    tparts = jnp.concatenate([thigh, thigh, tlow], 1)
    crossing = {}

    def leave(c):
        for copy in crossing[c]:
            copy.wait()
        for way in range(2):
            hop(way, 0, c)

    for c in range(4):

        def pair(p, carry):
            b = 8 * c + 2 * p
            both = jnp.where(lane < 64, one_block(b), one_block(b + 1))
            image[:, pl.ds(pl.multiple_of(p * 128, 128), 128)] = both
            return carry

        lax.fori_loop(0, 4, pair, 0, unroll=4)
        high, low = halves(image[...])
        ts = dot(tparts, jnp.concatenate([high, low, high], 0))
        for k in range(4):
            at = slice(128 * k, 128 * k + 128)
            tr, ti = ts[0:32, at], ts[32:64, at]
            other = jnp.where(sign < 0, pltpu.roll(ti, 96, 1), pltpu.roll(ti, 32, 1))
            tile[c, :, at] = tr + sign * other
        crossing[c] = [x_copy(c, d) for d in range(NX - 1)]
        for copy in crossing[c]:
            copy.start()
        own = pltpu.make_async_copy(
            tile.at[c, pl.ds(pl.multiple_of(x * 8, 8), 8)], tiles.at[z, c, x], keep.at[c]
        )
        own.start()
        crossing[c].append(own)
        if c:
            leave(c - 1)
    leave(3)

    last = NZ // 2 - 1
    for step in range(1, NZ // 2):
        for c in range(4):
            for way in range(2):
                sent[way, step - 1, c].wait_recv()
                if step < last or (c < 2) == (way == 0):
                    hop(way, step, c)
    for (way, step, c), copy in sent.items():
        if step == last:
            copy.wait_recv()
    for copy in sent.values():
        copy.wait_send()


def front(vis, off, gain, st, band, place):
    hbm = pl.BlockSpec(memory_space=pl.ANY)
    vmem = pl.BlockSpec(memory_space=pltpu.VMEM)
    dma = pltpu.SemaphoreType.DMA
    return pl.pallas_call(
        front_kernel,
        out_shape=[
            jax.ShapeDtypeStruct((NZ, 4, NX, 8, 512), F32),
            jax.ShapeDtypeStruct((NZ, 128), jnp.int32),
        ],
        in_specs=[hbm] * 7,
        out_specs=[hbm, vmem],
        scratch_shapes=[
            pltpu.VMEM((2, 4, 8, 256), F32),
            pltpu.VMEM((2, 4, 8, 256), F32),
            pltpu.VMEM((16, 512), F32),
            pltpu.VMEM((2, 256), jnp.int32),
            pltpu.VMEM((128, 128), jnp.int32),
            pltpu.VMEM((128, 128), jnp.int32),
            pltpu.VMEM((64, 32), F32),
            pltpu.VMEM((256, 128), F32),
            pltpu.VMEM((8, 32, 128), F32),
            pltpu.VMEM((4, 32, 256), F32),
            pltpu.VMEM((32, 512), F32),
            pltpu.VMEM((4, 32, 512), F32),
            dma((7,)),
            dma((4,)),
            dma((NCH - 1,)),
            dma((NCH - 1,)),
            dma((4, NX - 1)),
            dma((4, NX - 1)),
            dma((2, NZ // 2, 4)),
            dma((2, NZ // 2, 4)),
        ],
        compiler_params=pltpu.CompilerParams(
            collective_id=0, has_side_effects=True, vmem_limit_bytes=58 << 20
        ),
    )(vis, off, gain, st, band, place, jnp.asarray(front_table()))


def rows_kernel(
    tiles_hbm, where, utab_hbm, out,
    tiles, utab, phase, wtab, where_s, lhs, prod_a, prod_b, acc, load, fetch,
):
    z = lax.axis_index("bt") // NX
    loads = [
        pltpu.make_async_copy(utab_hbm.at[z], utab, load.at[0]),
        pltpu.make_async_copy(where, where_s, load.at[1]),
    ]

    def slot_copy(slot):
        return pltpu.make_async_copy(tiles_hbm.at[slot], tiles.at[slot], fetch.at[slot])

    slot_copy(0).start()
    for copy in loads:
        copy.start()
    for slot in range(1, NZ):
        slot_copy(slot).start()
    acc[...] = jnp.zeros_like(acc)
    low_half = lanes((8, 128)) < 64

    def build(slot):
        for c in range(4):
            for xs in range(NX):
                for p in range(4):
                    v = tiles[slot, c, xs, :, 128 * p : 128 * p + 128]
                    high = v.astype(BF).astype(F32)
                    rolled = pltpu.roll(v - high, 64, 1)
                    first = jnp.concatenate(
                        [jnp.where(low_half, high, rolled), jnp.where(low_half, high, 0.0)], 1
                    )
                    second = jnp.concatenate(
                        [jnp.where(low_half, rolled, high), jnp.where(low_half, 0.0, high)], 1
                    )
                    k = 256 * c + 64 * xs + 16 * p
                    lhs[k : k + 16, :] = jnp.concatenate([first, second], 0).astype(BF)

    def add_tile(slot, prod, c, b):
        word = where_s[slot, (b // 8) * 32 + c * 8 + b % 8]
        tr, tc = word >> 5, word & 31
        cs, sn = phase[pl.ds(tr, 1), 0:256], phase[pl.ds(tr, 1), 256:512]
        rows = pl.ds(pl.multiple_of(c * 256 + 8 * b, 8), 8)
        for h in range(2):
            re, im = slice(256 * h, 256 * h + 256), slice(512 + 256 * h, 768 + 256 * h)
            pr, pi = prod[rows, re], prod[rows, im]
            acc[tc, :, re] += cs * pr - sn * pi
            acc[tc, :, im] += cs * pi + sn * pr

    for k in range(4):
        tr = lax.broadcasted_iota(jnp.int32, (64, 256), 0) + 64 * k
        turns = (tr * lanes((64, 256)) % 256).astype(F32) * (1.0 / 256.0)
        phase[64 * k : 64 * k + 64, 0:256], phase[64 * k : 64 * k + 64, 256:512] = phasor(turns)
    slot_copy(0).wait()
    build(0)
    for copy in loads:
        copy.wait()
    uhigh, ulow = halves(utab[...])
    wtab[...] = jnp.concatenate([uhigh, uhigh, ulow, ulow], 0)
    prod_a[...] = dot(lhs[...], wtab[...])

    def two(m, carry):
        for slot, now, later in ((2 * m, prod_a, prod_b), (2 * m + 1, prod_b, prod_a)):
            following = jnp.minimum(slot + 1, NZ - 1)

            @pl.when(slot + 1 < NZ)
            def _():
                slot_copy(following).wait()

            build(following)

            def part(c, carry):
                at = pl.ds(pl.multiple_of(256 * c, 256), 256)
                later[:, at] = dot(lhs[...], wtab[:, at])
                for b in range(32):
                    add_tile(slot, now, c, b)
                return carry

            lax.fori_loop(0, 4, part, 0)
        return carry

    lax.fori_loop(0, NZ // 2, two, 0)

    for q in range(8):
        prod_a[32 * q : 32 * q + 32, :] = acc[:, q, :]
    for k in range(8):
        out[128 * k : 128 * k + 128, :] = prod_a[0:256, 128 * k : 128 * k + 128].T


def image_rows(tiles, where):
    hbm = pl.BlockSpec(memory_space=pl.ANY)
    vmem = pl.BlockSpec(memory_space=pltpu.VMEM)
    return pl.pallas_call(
        rows_kernel,
        out_shape=jax.ShapeDtypeStruct((1024, 256), F32),
        in_specs=[hbm] * 3,
        out_specs=vmem,
        scratch_shapes=[
            pltpu.VMEM((NZ, 4, NX, 8, 512), F32),
            pltpu.VMEM((64, 1024), F32),
            pltpu.VMEM((256, 512), F32),
            pltpu.VMEM((256, 1024), BF),
            pltpu.SMEM((NZ, 128), jnp.int32),
            pltpu.VMEM((1024, 256), BF),
            pltpu.VMEM((1024, 1024), F32),
            pltpu.VMEM((1024, 1024), F32),
            pltpu.VMEM((32, 8, 1024), F32),
            pltpu.SemaphoreType.DMA((2,)),
            pltpu.SemaphoreType.DMA((NZ,)),
        ],
        compiler_params=pltpu.CompilerParams(vmem_limit_bytes=52 << 20),
    )(tiles, where, jnp.asarray(row_table()))


def spread_kernel(rows, out, stage, local, send, recv, there, here, onward, landed):
    bt, ch = lax.axis_index("bt"), lax.axis_index("ch")
    z, x = bt // NX, bt % NX
    y, core = ch // 2, ch % 2
    me = x * NCH + ch

    def at(dx, dy, dc):
        xx, yy, cc = (x + dx) % NX, (y + dy) % 4, (core + dc) % 2
        return xx * NCH + 2 * yy + cc, (z * NX + xx, 2 * yy + cc)

    steps = [(dx, dy, dc) for dx in (2, 1, 3, 0) for dy in (2, 1, 3, 0) for dc in (0, 1)][:-2] + [(0, 0, 1)]
    around = [((2, dy, 1), (3, 0, 0), (1, 0, 0), (3, dy, 1)) for dy in range(4)]
    around += [((dx, 2, 0), (0, 3, 0), (0, 1, 0), (dx, 3, 0)) for dx in range(4)]
    straight = [step for step in steps if step not in [way[0] for way in around]]
    barrier = pltpu.get_barrier_semaphore()
    for step in steps:
        pl.semaphore_signal(barrier, inc=1, device_id=at(*step)[1], device_id_type=MESH)
    own = pltpu.make_async_copy(rows.at[:, me], out.at[me], local)
    own.start()
    pl.semaphore_wait(barrier, len(steps))

    def remote(src, dst, sender, receiver, peer):
        copy = pltpu.make_async_remote_copy(
            src_ref=src,
            dst_ref=dst,
            send_sem=sender,
            recv_sem=receiver,
            device_id=peer,
            device_id_type=MESH,
        )
        copy.start()
        return copy

    first = [
        remote(rows.at[:, at(*goal)[0]], stage.at[j], there.at[j], here.at[j], at(*relay)[1])
        for j, (goal, relay, _, _) in enumerate(around)
    ]
    copies = [
        remote(rows.at[:, at(*goal)[0]], out.at[me], send.at[j], recv.at[j], at(*goal)[1])
        for j, goal in enumerate(straight)
    ]
    for j, (_, _, origin, goal) in enumerate(around):
        first[j].wait_recv()
        copies.append(
            remote(stage.at[j], out.at[at(*origin)[0]], onward.at[j], landed.at[j], at(*goal)[1])
        )
    for copy in copies:
        copy.wait()
    for copy in first:
        copy.wait_send()
    own.wait()


def spread(rows):
    vmem = pl.BlockSpec(memory_space=pltpu.VMEM)
    n = NX * NCH
    dma = pltpu.SemaphoreType.DMA
    return pl.pallas_call(
        spread_kernel,
        out_shape=jax.ShapeDtypeStruct((n, 2, 16, 256), F32),
        in_specs=[vmem],
        out_specs=vmem,
        scratch_shapes=[
            pltpu.VMEM((8, 2, 16, 256), F32),
            dma,
            dma((n - 9,)),
            dma((n - 9,)),
            dma((8,)),
            dma((8,)),
            dma((8,)),
            dma((8,)),
        ],
        compiler_params=pltpu.CompilerParams(
            collective_id=1, has_side_effects=True, vmem_limit_bytes=40 << 20
        ),
    )(rows)


def turn(values):
    n = len(values)
    if n == 1:
        return values
    even, odd = turn(values[0::2]), turn(values[1::2])
    low, high = [], []
    for k in range(n // 2):
        er, ei = even[k]
        xr, xi = odd[k]
        if k == 0:
            tr, ti = xr, xi
        elif 4 * k == n:
            tr, ti = -xi, xr
        else:
            c, s = math.cos(2 * math.pi * k / n), math.sin(2 * math.pi * k / n)
            tr, ti = c * xr - s * xi, c * xi + s * xr
        low.append((er + tr, ei + ti))
        high.append((er - tr, ei - ti))
    return low + high


def columns_kernel(parts, table, twiddle, out, whigh, wlow, vhigh, vlow, mid):
    c, s = table[:, 0:256], table[:, 256:512]
    for rows, both in ((slice(0, 256), table[...]), (slice(256, 512), jnp.concatenate([-s, c], 1))):
        whigh[rows, :], wlow[rows, :] = halves(both)
    lane = lanes((16, 128))

    def one_x(x, carry):
        for r in range(2):
            for h in range(2):
                for j in range(2):
                    pieces = [parts[x * 8 + 4 * h + i, r, :, 128 * j : 128 * j + 128] for i in range(4)]
                    for jj in range(4):
                        got = None
                        for i in range(4):
                            shift = (32 * (i - jj)) % 128
                            piece = pltpu.roll(pieces[i], shift, 1) if shift else pieces[i]
                            got = piece if got is None else jnp.where(lane >= 32 * i, piece, got)
                        high, low = halves(got)
                        rows = pl.ds(pl.multiple_of((x * 8 + 4 * j + jj) * 16, 16), 16)
                        at = slice(256 * r + 128 * h, 256 * r + 128 * h + 128)
                        vhigh[rows, at] = high
                        vlow[rows, at] = low
        return carry

    lax.fori_loop(0, NX, one_x, 0)
    mid[...] = dot(vhigh[...], whigh[...]) + (dot(vlow[...], whigh[...]) + dot(vhigh[...], wlow[...]))
    for a in range(2):
        for e in range(2):
            values = []
            for q in range(SUB):
                rows = slice(16 * q + 8 * a, 16 * q + 8 * a + 8)
                zr = mid[rows, 128 * e : 128 * e + 128]
                zi = mid[rows, 256 + 128 * e : 384 + 128 * e]
                c = twiddle[q : q + 1, 128 * e : 128 * e + 128]
                s = twiddle[q : q + 1, 256 + 128 * e : 384 + 128 * e]
                values.append((c * zr - s * zi, c * zi + s * zr))
            for k, (re, im) in enumerate(turn(values)):
                at = slice(256 * k + 128 * e, 256 * k + 128 * e + 128)
                out[0, 8 * a : 8 * a + 8, at] = re
                out[1, 8 * a : 8 * a + 8, at] = im


def columns(parts):
    vmem = pl.BlockSpec(memory_space=pltpu.VMEM)
    return pl.pallas_call(
        columns_kernel,
        out_shape=jax.ShapeDtypeStruct((2, 16, G), F32),
        in_specs=[vmem] * 3,
        out_specs=vmem,
        scratch_shapes=[
            pltpu.VMEM((512, 512), BF),
            pltpu.VMEM((512, 512), BF),
            pltpu.VMEM((512, 512), BF),
            pltpu.VMEM((512, 512), BF),
            pltpu.VMEM((512, 512), F32),
        ],
        compiler_params=pltpu.CompilerParams(vmem_limit_bytes=40 << 20),
    )(parts, jnp.asarray(column_table()), jnp.asarray(column_twiddle()))


def shards(visibility, cell_offset, station_gain, stations, row_band, tile_offset):
    tiles, where = front(
        visibility,
        cell_offset,
        station_gain.reshape(16, 512),
        stations.T,
        row_band.reshape(128, 128),
        tile_offset.reshape(128, 128),
    )
    rows = image_rows(tiles, where)
    return columns(spread(rows.reshape(2, NX * NCH, 16, 256)))


def solution(mesh):
    return jax.shard_map(
        shards,
        mesh=mesh,
        in_specs=(
            P(None, None, "ch", "bt"),
            P(None, None, "ch", "bt"),
            P(None, "ch", None),
            P("bt", None),
            P(),
            P(),
        ),
        out_specs=P(None, ("bt", "ch"), None),
        check_vma=False,
    )
```

time: 160 us -> 123 us (0.77)
  Pallas kernels: 149 us -> 122 us
  local copies, waits for them, and re-layouts: 8.55 us -> 0.7 us
  other arithmetic: 1.75 us -> 0 us
    pallas_call x1, Pallas kernels: 46.6 us -> 26.5 us  [image_rows(): pl.pallas_call(rows_kernel, out_shape=jax.ShapeDtypeStruct((1024, 256), F...]
    pallas_call x1, Pallas kernels: 77.1 us -> 69.4 us  [front(): pl.pallas_call(front_kernel, out_shape=[jax.ShapeDtypeStruct((NZ, 4, NX,...]
    unnamed x20 -> x6, local copies, waits for them, and re-layouts: 8.27 us -> 0.7 us
where the time goes in v2:
time: 123 us
  Pallas kernels  122 us (99%)
    pallas_call x1, Pallas kernels, front(): pl.pallas_call(front_kernel, out_shape=[jax.ShapeDtypeStruct((NZ, 4, NX,...  69.4 us
    pallas_call x1, Pallas kernels, image_rows(): pl.pallas_call(rows_kernel, out_shape=jax.ShapeDtypeStruct((1024, 256), F...  26.5 us
    pallas_call x1, Pallas kernels, spread(): pl.pallas_call(spread_kernel, out_shape=jax.ShapeDtypeStruct((n, 2, 16, 2...  22.6 us
    pallas_call x1, Pallas kernels, columns(): pl.pallas_call(columns_kernel, out_shape=jax.ShapeDtypeStruct((2, 16, G),...  3.51 us

profile of v2, /device:TPU:1, one launch (start us, length us, event | category | flops | bytes accessed | tf_op | source)
XLA Modules:
  0.0 122.7 jit_solution(792536739666360418)
XLA Ops:
  0.0 69.4 %shard_map.100 = (f32[16,4,4,8,512]{4,3,2,1,0:T(8,128)}, s32[16,128]{1,0:T(8,128)}) custom-call(f32[2,4,8,256]{3,2,1,0:T(8,128)} %vis_hbm.1, f32[2,4,8,256]{3,2,1,0:T(8,128)} %off_hbm.1, f32[16,512]{1,0:T(8,128)} %bitcast.8, s32[2,256]{1,0:T(2,128)} %bitcast.9, s32[128,128]{1,0:T(8,128)} %bitcast.6, s32[128,128]{1,0:T(8,128)} %bitcast.7, ...), custom_call_target="tpu_custom_call" | custom-call | tf_op jit(solution)/shard_map/pallas_call | solution.py:315
  69.4 0.0 copy-start.2
  69.4 0.7 copy-done.2
  70.1 0.0 copy-start
  70.1 0.0 copy-start.1
  70.1 26.5 %shard_map.101 = f32[1024,256]{1,0:T(8,128)S(1)} custom-call(f32[16,4,4,8,512]{4,3,2,1,0:T(8,128)} %get-tuple-element.7.tiles_hbm, s32[16,128]{1,0:T(8,128)S(1)} %copy-done.2, f32[16,64,1024]{2,1,0:T(8,128)} %constant.9.clone.utab_hbm), custom_call_target="tpu_custom_call" | custom-call | tf_op jit(solution)/shard_map/pallas_call | solution.py:442
  96.5 22.6 %shard_map.102.parts = f32[32,2,16,256]{3,2,1,0:T(8,128)S(1)} custom-call(f32[2,32,16,256]{3,2,1,0:T(8,128)S(1)} %bitcast.5), custom_call_target="tpu_custom_call" | custom-call | tf_op jit(solution)/shard_map/pallas_call | solution.py:521
  119.2 0.0 copy-done
  119.2 0.0 copy-done.1
  119.2 3.5 %shard_map.103 = f32[2,16,8192]{2,1,0:T(8,128)} custom-call(f32[32,2,16,256]{3,2,1,0:T(8,128)S(1)} %shard_map.102.parts, f32[256,512]{1,0:T(8,128)S(1)} %copy-done, f32[32,512]{1,0:T(8,128)S(1)} %copy-done.1), custom_call_target="tpu_custom_call" | custom-call | tf_op jit(solution)/shard_map/pallas_call | solution.py:607
Async XLA Ops:
  69.4 0.7 copy-start.2
  70.1 49.1 %copy-start = (f32[256,512]{1,0:T(8,128)S(1)}, f32[256,512]{1,0:T(8,128)}, u32[]{:S(2)}) copy-start(f32[256,512]{1,0:T(8,128)} %constant.10.clone.table) | copy-start | bytes 1572868
  70.1 49.1 %copy-start.1 = (f32[32,512]{1,0:T(8,128)S(1)}, f32[32,512]{1,0:T(8,128)}, u32[]{:S(2)}) copy-start(f32[32,512]{1,0:T(8,128)} %constant.11.clone.twiddle) | copy-start | bytes 196612

commit v3 on v2

--- a/solution.py
+++ b/solution.py
@@ -408,27 +408,32 @@
     wtab[...] = jnp.concatenate([uhigh, uhigh, ulow, ulow], 0)
     prod_a[...] = dot(lhs[...], wtab[...])
 
+    def one(slot, now, later):
+        slot_copy(slot + 1).wait()
+        build(slot + 1)
+
+        def part(c, carry):
+            at = pl.ds(pl.multiple_of(256 * c, 256), 256)
+            later[:, at] = dot(lhs[...], wtab[:, at])
+            for b in range(32):
+                add_tile(slot, now, c, b)
+            return carry
+
+        lax.fori_loop(0, 4, part, 0)
+
     def two(m, carry):
-        for slot, now, later in ((2 * m, prod_a, prod_b), (2 * m + 1, prod_b, prod_a)):
-            following = jnp.minimum(slot + 1, NZ - 1)
-
-            @pl.when(slot + 1 < NZ)
-            def _():
-                slot_copy(following).wait()
-
-            build(following)
-
-            def part(c, carry):
-                at = pl.ds(pl.multiple_of(256 * c, 256), 256)
-                later[:, at] = dot(lhs[...], wtab[:, at])
-                for b in range(32):
-                    add_tile(slot, now, c, b)
-                return carry
-
-            lax.fori_loop(0, 4, part, 0)
+        one(2 * m, prod_a, prod_b)
+        one(2 * m + 1, prod_b, prod_a)
         return carry
 
-    lax.fori_loop(0, NZ // 2, two, 0)
+    def final(c, carry):
+        for b in range(32):
+            add_tile(NZ - 1, prod_b, c, b)
+        return carry
+
+    lax.fori_loop(0, NZ // 2 - 1, two, 0)
+    one(NZ - 2, prod_a, prod_b)
+    lax.fori_loop(0, 4, final, 0)
 
     for q in range(8):
         prod_a[32 * q : 32 * q + 32, :] = acc[:, q, :]

time: 123 us -> 122 us (level)
  no operation moved by 1% of the time
where the time goes in v3:
time: 122 us
  Pallas kernels  121 us (99%)
    pallas_call x1, Pallas kernels, front(): pl.pallas_call(front_kernel, out_shape=[jax.ShapeDtypeStruct((NZ, 4, NX,...  69.4 us
    pallas_call x1, Pallas kernels, image_rows(): pl.pallas_call(rows_kernel, out_shape=jax.ShapeDtypeStruct((1024, 256), F...  25.9 us
    pallas_call x1, Pallas kernels, spread(): pl.pallas_call(spread_kernel, out_shape=jax.ShapeDtypeStruct((n, 2, 16, 2...  22.6 us
    pallas_call x1, Pallas kernels, columns(): pl.pallas_call(columns_kernel, out_shape=jax.ShapeDtypeStruct((2, 16, G),...  3.51 us

profile of v3, /device:TPU:1, one launch (start us, length us, event | category | flops | bytes accessed | tf_op | source)
XLA Modules:
  0.0 122.1 jit_solution(7065061021776770612)
XLA Ops:
  0.0 69.4 %shard_map.100 = (f32[16,4,4,8,512]{4,3,2,1,0:T(8,128)}, s32[16,128]{1,0:T(8,128)}) custom-call(f32[2,4,8,256]{3,2,1,0:T(8,128)} %vis_hbm.1, f32[2,4,8,256]{3,2,1,0:T(8,128)} %off_hbm.1, f32[16,512]{1,0:T(8,128)} %bitcast.8, s32[2,256]{1,0:T(2,128)} %bitcast.9, s32[128,128]{1,0:T(8,128)} %bitcast.6, s32[128,128]{1,0:T(8,128)} %bitcast.7, ...), custom_call_target="tpu_custom_call" | custom-call | tf_op jit(solution)/shard_map/pallas_call | solution.py:315
  69.4 0.0 copy-start.2
  69.4 0.7 copy-done.2
  70.1 0.0 copy-start
  70.1 0.0 copy-start.1
  70.1 25.9 %shard_map.101 = f32[1024,256]{1,0:T(8,128)S(1)} custom-call(f32[16,4,4,8,512]{4,3,2,1,0:T(8,128)} %get-tuple-element.7.tiles_hbm, s32[16,128]{1,0:T(8,128)S(1)} %copy-done.2, f32[16,64,1024]{2,1,0:T(8,128)} %constant.9.clone.utab_hbm), custom_call_target="tpu_custom_call" | custom-call | tf_op jit(solution)/shard_map/pallas_call | solution.py:447
  96.0 22.6 %shard_map.102.parts = f32[32,2,16,256]{3,2,1,0:T(8,128)S(1)} custom-call(f32[2,32,16,256]{3,2,1,0:T(8,128)S(1)} %bitcast.5), custom_call_target="tpu_custom_call" | custom-call | tf_op jit(solution)/shard_map/pallas_call | solution.py:526
  118.6 0.0 copy-done
  118.6 0.0 copy-done.1
  118.6 3.5 %shard_map.103 = f32[2,16,8192]{2,1,0:T(8,128)} custom-call(f32[32,2,16,256]{3,2,1,0:T(8,128)S(1)} %shard_map.102.parts, f32[256,512]{1,0:T(8,128)S(1)} %copy-done, f32[32,512]{1,0:T(8,128)S(1)} %copy-done.1), custom_call_target="tpu_custom_call" | custom-call | tf_op jit(solution)/shard_map/pallas_call | solution.py:612
Async XLA Ops:
  69.4 0.7 copy-start.2
  70.1 48.5 %copy-start = (f32[256,512]{1,0:T(8,128)S(1)}, f32[256,512]{1,0:T(8,128)}, u32[]{:S(2)}) copy-start(f32[256,512]{1,0:T(8,128)} %constant.10.clone.table) | copy-start | bytes 1572868
  70.1 48.6 %copy-start.1 = (f32[32,512]{1,0:T(8,128)S(1)}, f32[32,512]{1,0:T(8,128)}, u32[]{:S(2)}) copy-start(f32[32,512]{1,0:T(8,128)} %constant.11.clone.twiddle) | copy-start | bytes 196612

commit v4 on v3

--- a/solution.py
+++ b/solution.py
@@ -183,8 +183,10 @@
     lane16 = lanes((NZ, 128))
     where = None
     for xs in range(NX):
-        at = pl.ds(2 * xs + ch // 4, NZ, stride=8)
-        piece = band[at, :] * 128 + place[at, :]
+        near, far = pl.ds(2 * xs, NZ, stride=8), pl.ds(2 * xs + 1, NZ, stride=8)
+        piece = jnp.where(
+            ch // 4 == 0, band[near, :] * 128 + place[near, :], band[far, :] * 128 + place[far, :]
+        )
         piece = pltpu.roll(piece, (32 * xs + 128 - 32 * (ch % 4)) % 128, 1)
         where = piece if where is None else jnp.where(lane16 >= 32 * xs, piece, where)
     where_out[...] = where

time: 122 us -> 122 us (level)
  no operation moved by 1% of the time
where the time goes in v4:
time: 122 us
  Pallas kernels  121 us (99%)
    pallas_call x1, Pallas kernels, front(): pl.pallas_call(front_kernel, out_shape=[jax.ShapeDtypeStruct((NZ, 4, NX,...  69.4 us
    pallas_call x1, Pallas kernels, image_rows(): pl.pallas_call(rows_kernel, out_shape=jax.ShapeDtypeStruct((1024, 256), F...  26 us
    pallas_call x1, Pallas kernels, spread(): pl.pallas_call(spread_kernel, out_shape=jax.ShapeDtypeStruct((n, 2, 16, 2...  22.6 us
    pallas_call x1, Pallas kernels, columns(): pl.pallas_call(columns_kernel, out_shape=jax.ShapeDtypeStruct((2, 16, G),...  3.51 us

profile of v4, /device:TPU:1, one launch (start us, length us, event | category | flops | bytes accessed | tf_op | source)
XLA Modules:
  0.0 122.2 jit_solution(6179137269824442032)
XLA Ops:
  0.0 69.4 %shard_map.100 = (f32[16,4,4,8,512]{4,3,2,1,0:T(8,128)}, s32[16,128]{1,0:T(8,128)}) custom-call(f32[2,4,8,256]{3,2,1,0:T(8,128)} %vis_hbm.1, f32[2,4,8,256]{3,2,1,0:T(8,128)} %off_hbm.1, f32[16,512]{1,0:T(8,128)} %bitcast.8, s32[2,256]{1,0:T(2,128)} %bitcast.9, s32[128,128]{1,0:T(8,128)} %bitcast.6, s32[128,128]{1,0:T(8,128)} %bitcast.7, ...), custom_call_target="tpu_custom_call" | custom-call | tf_op jit(solution)/shard_map/pallas_call | solution.py:317
  69.4 0.0 copy-start.2
  69.4 0.7 copy-done.2
  70.1 0.0 copy-start
  70.1 0.0 copy-start.1
  70.1 26.0 %shard_map.101 = f32[1024,256]{1,0:T(8,128)S(1)} custom-call(f32[16,4,4,8,512]{4,3,2,1,0:T(8,128)} %get-tuple-element.7.tiles_hbm, s32[16,128]{1,0:T(8,128)S(1)} %copy-done.2, f32[16,64,1024]{2,1,0:T(8,128)} %constant.9.clone.utab_hbm), custom_call_target="tpu_custom_call" | custom-call | tf_op jit(solution)/shard_map/pallas_call | solution.py:449
  96.0 22.6 %shard_map.102.parts = f32[32,2,16,256]{3,2,1,0:T(8,128)S(1)} custom-call(f32[2,32,16,256]{3,2,1,0:T(8,128)S(1)} %bitcast.5), custom_call_target="tpu_custom_call" | custom-call | tf_op jit(solution)/shard_map/pallas_call | solution.py:528
  118.7 0.0 copy-done
  118.7 0.0 copy-done.1
  118.7 3.5 %shard_map.103 = f32[2,16,8192]{2,1,0:T(8,128)} custom-call(f32[32,2,16,256]{3,2,1,0:T(8,128)S(1)} %shard_map.102.parts, f32[256,512]{1,0:T(8,128)S(1)} %copy-done, f32[32,512]{1,0:T(8,128)S(1)} %copy-done.1), custom_call_target="tpu_custom_call" | custom-call | tf_op jit(solution)/shard_map/pallas_call | solution.py:614
Async XLA Ops:
  69.4 0.7 copy-start.2
  70.1 48.6 %copy-start = (f32[256,512]{1,0:T(8,128)S(1)}, f32[256,512]{1,0:T(8,128)}, u32[]{:S(2)}) copy-start(f32[256,512]{1,0:T(8,128)} %constant.10.clone.table) | copy-start | bytes 1572868
  70.1 48.6 %copy-start.1 = (f32[32,512]{1,0:T(8,128)S(1)}, f32[32,512]{1,0:T(8,128)}, u32[]{:S(2)}) copy-start(f32[32,512]{1,0:T(8,128)} %constant.11.clone.twiddle) | copy-start | bytes 196612
